TPU v7x, 32 devices: a whole 2x2x4 slice. The times are simulated.
32 devices in a mesh: section: 2 (over core), dp: 16 (over z, y, x).
Axes of the slice: x: 2, y: 2, z: 4, core: 2. Of those that a mesh axis runs over, the one named last changes fastest.
Arguments:
- node_input: bfloat16 [32768, 256], P('dp'), may hold values from -6 to 6
- edge_input: bfloat16 [262144, 256], P('dp'), may hold values from -6 to 6
- senders: int32 [262144], P('dp'), may hold values from 0 to 511
- receivers: int32 [262144], P('dp'), may hold values from 0 to 511
- node_cot: bfloat16 [32768, 256], P('dp'), may hold values from -6 to 6
- edge_cot: bfloat16 [262144, 256], P('dp'), may hold values from -6 to 6
- edge_w1: bfloat16 [2, 768, 256], P('section'), may hold values from -0.21875 to 0.21875
- edge_b1: float32 [2, 256], P('section'), may hold values from -3 to 3
- edge_w2: bfloat16 [2, 256, 256], P('section'), may hold values from -0.375 to 0.375
- edge_b2: float32 [2, 256], P('section'), may hold values from -3 to 3
- edge_gain: float32 [2, 256], P('section'), may hold values from 0.5 to 1.5
- edge_shift: float32 [2, 256], P('section'), may hold values from -3 to 3
- node_w1: bfloat16 [2, 512, 256], P('section'), may hold values from -0.25 to 0.25
- node_b1: float32 [2, 256], P('section'), may hold values from -3 to 3
- node_w2: bfloat16 [2, 256, 256], P('section'), may hold values from -0.375 to 0.375
- node_b2: float32 [2, 256], P('section'), may hold values from -3 to 3
- node_gain: float32 [2, 256], P('section'), may hold values from 0.5 to 1.5
- node_shift: float32 [2, 256], P('section'), may hold values from -3 to 3
Outputs:
- node_latents: float32 [2, 32768, 256], P('section', 'dp')
- edge_latents: float32 [2, 262144, 256], P('section', 'dp')
- node_grads: float32 [2, 32768, 256], P('section', 'dp')
- edge_grads: float32 [2, 262144, 256], P('section', 'dp')
- grad_edge_w1: float32 [2, 768, 256], P('section')
- grad_edge_b1: float32 [2, 256], P('section')
- grad_edge_w2: float32 [2, 256, 256], P('section')
- grad_edge_b2: float32 [2, 256], P('section')
- grad_edge_gain: float32 [2, 256], P('section')
- grad_edge_shift: float32 [2, 256], P('section')
- grad_node_w1: float32 [2, 512, 256], P('section')
- grad_node_b1: float32 [2, 256], P('section')
- grad_node_w2: float32 [2, 256, 256], P('section')
- grad_node_b2: float32 [2, 256], P('section')
- grad_node_gain: float32 [2, 256], P('section')
- grad_node_shift: float32 [2, 256], P('section')
Inputs may be any that keep to these rules, and one draw needn't show every extreme that they name: `senders`: indices within the edge's own graph of 512 nodes. `receivers`: indices within the edge's own graph of 512 nodes.
All inputs are finite; a program needn't handle non-finite values.
Results may differ from a plain program's by a relative error of at most 0.019.
Values may be sent and summed in bfloat16 or wider, within the bound.
No kernel may reach another device: no remote copies, remote signals or barrier semaphores. Data moves between devices by JAX's collectives and lax.ppermute only.
A program may use at most 320 MiB of HBM per device.

v0:
```python
import functools

import jax
import jax.numpy as jnp
from jax import lax
from jax.experimental import pallas as pl
from jax.experimental.pallas import tpu as pltpu
from jax.sharding import PartitionSpec as P

MICRO = 4
GRAPHS = 2
EPS = 1e-05
BLOCK = 256
NODE_BLOCKS = 1
CHUNK = 1024
GRAD_ROWS = 1856
F32 = jnp.float32
BF16 = jnp.bfloat16


def dot(left, right):
    return jnp.dot(left, right, preferred_element_type=F32)


def dot_tn(left, right):
    return lax.dot_general(left, right, (((0,), (0,)), ((), ())), preferred_element_type=F32)


def dot_nt(left, right):
    return lax.dot_general(left, right, (((1,), (1,)), ((), ())), preferred_element_type=F32)


def col_sum(value):
    return jnp.sum(value, axis=0, keepdims=True)


def row_mean(value):
    return jnp.mean(value, axis=1, keepdims=True)


def half_silu(half):
    t = jnp.tanh(half)
    up = 1.0 + t
    act = half * up
    return act, up + act * (1.0 - t)


def twice(lanes):
    return jnp.concatenate([lanes, lanes], axis=1)


def eight_rows(value):
    return jnp.sum(value.reshape(-1, 8, value.shape[1]), axis=0)


def centre(w):
    w = w.astype(F32)
    return (w - row_mean(w)).astype(BF16)


def interleave(parts, skew):
    parts = list(parts)
    done = [False] * len(parts)
    clock = 0
    while not all(done):
        for i, part in enumerate(parts):
            if clock >= i * skew and not done[i]:
                done[i] = next(part, "end") == "end"
        clock += 1


def graphs_kernel(
    nodes,
    edges,
    width,
    sec_ref,
    idx_s,
    idx_r,
    node_hbm,
    edge_hbm,
    ncot_hbm,
    ecot_hbm,
    w_mine,
    w_theirs,
    v_mine,
    v_theirs,
    lat_e,
    lat_n,
    gr_e,
    gr_n,
    send_e,
    send_n,
    wg_keep,
    wg_send,
    es,
    srt,
    cot,
    low,
    act0,
    act1,
    dd0,
    dd1,
    xh0,
    xh1,
    inv0,
    inv1,
    big,
    wv,
    wc,
    vs,
    h0_in,
    cotn,
    nf,
    nlow,
    acc,
    dh_own,
    pw,
    jn,
    act_n,
    slope_n,
    xh_n,
    inv_n,
    wg,
    load_sems,
    big_sems,
    node_sems,
    low_sems,
    nlow_sems,
    grad_sems,
):
    acts, dds, xhs, invs = (act0, act1), (dd0, dd1), (xh0, xh1), (inv0, inv1)
    sec = sec_ref[0]
    first = sec == 0
    n = BLOCK
    rows_n = nodes // NODE_BLOCKS
    node_rows = [slice(i * rows_n, (i + 1) * rows_n) for i in range(NODE_BLOCKS)]
    col_s, col_r, col_1 = width, width + nodes, width + 2 * nodes
    spans = (slice(0, col_1), slice(col_s, col_1 + width))
    own = (slice(0, width), slice(col_1, col_1 + width))
    copy = pltpu.make_async_copy
    rounds = (0, 1, 1, 0)
    full = ((lat_e, lat_n), (lat_e, lat_n), (gr_e, gr_n), (gr_e, gr_n))
    lows = (es.at[:, own[1]], low, low, cot)

    @pl.when(first)
    def _():
        copy(w_mine, wv.at[0], load_sems.at[4]).start()
        copy(w_theirs, wv.at[1], load_sems.at[5]).start()

    @pl.when(jnp.logical_not(first))
    def _():
        copy(w_theirs, wv.at[0], load_sems.at[4]).start()
        copy(w_mine, wv.at[1], load_sems.at[5]).start()

    vs[0] = jnp.where(first, v_mine[...], v_theirs[...])
    vs[1] = jnp.where(first, v_theirs[...], v_mine[...])
    wg[...] = jnp.zeros_like(wg)

    def vec(r, k):
        return vs[r, k : k + 1, :]

    def weights(r):
        w1 = [wv[r, k * width : (k + 1) * width, :] for k in range(3)]
        at = 3 * width
        return (
            w1[0],
            jnp.concatenate(w1[1:], axis=1),
            wv[r, at : at + width, :],
            wv[r, at + width : at + 3 * width, :],
            wv[r, at + 3 * width : at + 4 * width, :],
        )

    def put_w(r, at, value):
        here = slice(at, at + value.shape[0])
        wg[r, here, :] = wg[r, here, :] + value

    def put_v(r, k, value):
        put_w(r, 7 * width + k, value)

    def graph(which, carry):
        gi = 2 * sec + which
        other = 2 * (1 - sec) + which
        erow = pl.multiple_of(gi * edges, edges)
        nrow = pl.multiple_of(gi * nodes, nodes)

        def big_copy(phase, k):
            at = pl.multiple_of(jnp.where(sec == rounds[phase], gi, other) * edges, edges) + k * CHUNK
            here = pl.ds(pl.multiple_of(at, CHUNK), CHUNK)
            return copy(big.at[pl.ds(k * CHUNK, CHUNK)], full[phase][0].at[here], big_sems.at[k])

        def big_wait(phase):
            for k in range(edges // CHUNK):
                big_copy(phase, k).wait()

        def node_copy(phase):
            at = pl.multiple_of(jnp.where(sec == rounds[phase], gi, other) * nodes, nodes)
            return copy(nf.at[phase % 2], full[phase][1].at[pl.ds(at, nodes)], node_sems.at[phase])

        def low_copies(phase):
            kind = jnp.where(sec == 0, 0, 1) if phase == 1 else phase // 2
            return (
                copy(lows[phase], send_e.at[kind, which], low_sems.at[phase]),
                copy(nlow.at[phase % 2], send_n.at[kind, which], nlow_sems.at[phase]),
            )

        def low_start(phase, k):
            if phase > 0 and (phase, k) != (2, 0):
                low_copies(phase - 1)[k].wait()
            if phase < 3:
                low_copies(phase)[k].start()
            else:

                @pl.when(sec != rounds[phase])
                def _():
                    low_copies(phase)[k].start()

        def nodes_out(phase, here, out):
            nf[phase % 2, here, :] = out
            nlow[phase % 2, here, :] = out.astype(BF16)

        def drain():
            big_wait(3)
            for phase in (2, 3):
                node_copy(phase).wait()

            @pl.when(sec != rounds[3])
            def _():
                for c in low_copies(3):
                    c.wait()

        loads = [
            copy(edge_hbm.at[pl.ds(erow, edges)], es.at[:, own[0]], load_sems.at[0]),
            copy(node_hbm.at[pl.ds(nrow, nodes)], h0_in, load_sems.at[1]),
            copy(ncot_hbm.at[pl.ds(nrow, nodes)], cotn, load_sems.at[3]),
        ]
        load_cot = copy(ecot_hbm.at[pl.ds(erow, edges)], cot, load_sems.at[2])
        for c in loads:
            c.start()

        rows = edges // 128
        irow = pl.multiple_of(gi * rows, rows)

        one, zero = jnp.ones((128, 128), BF16), jnp.zeros((128, 128), BF16)

        def build(j):
            at = slice(j * 128, (j + 1) * 128)
            for k, idx in enumerate((idx_s, idx_r)):
                row = idx[pl.ds(irow + j, 1), :]
                ahead = jnp.broadcast_to(row, (16, 128)) - lax.broadcasted_iota(jnp.int32, (16, 128), 0)
                ahead = ahead.astype(jnp.int16)
                for c in range(0, nodes, 16):
                    hit = jnp.where(ahead == jnp.int16(c), one[:16], zero[:16])
                    srt[k * nodes + c : k * nodes + c + 16, at] = hit
                column = jnp.broadcast_to(row, (128, 128)).T
                ahead = (column - lax.broadcasted_iota(jnp.int32, (128, 128), 1)).astype(jnp.int16)
                for c in range(0, nodes, 128):
                    to = col_s + k * nodes + c
                    es[at, to : to + 128] = jnp.where(ahead == jnp.int16(c), one, zero)

        @pl.when(which == 0)
        def _():
            copy(w_mine, wv.at[0], load_sems.at[4]).wait()
            copy(w_mine, wv.at[1], load_sems.at[5]).wait()
            for r in range(2):
                we, _, w2, _, w4 = weights(r)
                wc[r, :width, :] = centre(w2)
                wc[r, width : 2 * width, :] = centre(w4)
                wc[r, 2 * width : 3 * width, :] = (w2.astype(F32) * 0.5).T.astype(BF16)
                wc[r, 3 * width :, :] = we.astype(F32).T.astype(BF16)

        @pl.when(which > 0)
        def _():
            drain()

        for c in loads:
            c.wait()

        def forward_table(r, here, h):
            _, wsr, _, _, _ = weights(r)
            hl = h.astype(BF16)
            jn[r, here, :width] = hl
            k_s = width if r == 0 else 0
            table = dot(hl, wsr) * 0.5
            pw[k_s + here.start : k_s + here.stop, :] = table[:, :width].astype(BF16)
            to = k_s + nodes
            pw[to + here.start : to + here.stop, :] = (table[:, width:] + vec(r, 0) * 0.5).astype(BF16)

        def forward(r, h):
            phase = r
            we, _, _, w3, _ = weights(r)
            k_e = 0 if r == 0 else 2 * nodes
            pw[k_e : k_e + width, :] = we * 0.5
            if r == 0:
                for here in node_rows:
                    forward_table(0, here, h(here))
            b2 = vec(r, 1)
            b2c = b2 - row_mean(b2)
            gain, shift = vec(r, 2), vec(r, 3)
            lo = lows[phase]
            message = (xh1, cot)[r]
            if phase > 0:
                big_wait(phase - 1)

            def block(i):
                here = slice(i * n, (i + 1) * n)
                if r == 0:
                    for j in range(i * n // 128, (i + 1) * n // 128):
                        build(j)
                    yield
                half = dot(es[here, spans[r]], pw[...])
                yield
                act, slope = half_silu(half)
                act = act.astype(BF16)
                acts[r][:, here] = act.T
                dds[r][here, :] = slope.astype(BF16)
                yield
                z = dot(act, wc[r, :width, :])
                yield
                z = z + b2c
                inv = lax.rsqrt(row_mean(z * z) + EPS)
                xh = z * inv
                xhs[r][here, :] = xh.astype(BF16)
                invs[r][here, :] = jnp.broadcast_to(inv, (n, 128)).astype(BF16)
                update = xh * gain + shift
                message[here, :] = update.astype(BF16)
                out = es[here, own[r]].astype(F32) + update
                big[here, :] = out
                lo[here, :] = out.astype(BF16)
                yield
                if (i + 1) * n % CHUNK == 0:
                    part = slice((i + 1) * n - CHUNK, (i + 1) * n)
                    big_copy(phase, i * n // CHUNK).start()
                    add = dot(srt[nodes:, part], message[part, :])
                    acc[:nodes, :] = add if part.start == 0 else acc[:nodes, :] + add
                    yield

            interleave([block(i) for i in range(edges // n)], 1)
            low_start(phase, 0)
            if r == 1:
                load_cot.start()
            b4 = vec(r, 5)
            b4c = b4 - row_mean(b4)
            b3 = vec(r, 4)

            def node_block(here):
                jn[r, here, width:] = acc[here, :].astype(BF16)
                z = dot(jn[r, here, :], w3)
                yield
                act, slope = half_silu((z + b3) * 0.5)
                act = act.astype(BF16)
                act_n[r, here, :] = act
                slope_n[r, here, :] = slope.astype(BF16)
                z = dot(act, wc[r, width : 2 * width, :])
                yield
                z = z + b4c
                inv = lax.rsqrt(row_mean(z * z) + EPS)
                xh = z * inv
                xh_n[r, here, :] = xh.astype(BF16)
                inv_n[r, here, :] = jnp.broadcast_to(inv, (rows_n, 128))
                out = h(here) + xh * vec(r, 6) + vec(r, 7)
                nodes_out(phase, here, out)
                if r == 0:
                    forward_table(1, here, out)
                yield

            interleave([node_block(here) for here in node_rows], 1)
            node_copy(phase).start()
            low_start(phase, 1)

        def backward(r, de_ref, dn_rows, before):
            phase = 3 - r
            _, wsr, _, w3, w4 = weights(r)
            gain_n = vec(r, 6)
            dns, d4s, d3s, djs = [], [], [], []

            def node_block(here):
                dn = dn_rows(here)
                dns.append(dn)
                yield
                xh = xh_n[r, here, :].astype(F32)
                g = dn * gain_n
                d4 = twice(inv_n[r, here, :]) * (g - row_mean(g) - xh * row_mean(g * xh))
                d4s.append(d4.astype(BF16))
                d3 = dot_nt(d4s[-1], w4)
                yield
                d3s.append((d3 * slope_n[r, here, :].astype(F32) * 0.5).astype(BF16))
                djn = dot_nt(d3s[-1], w3)
                yield
                djs.append(djn[:, width:].astype(BF16))
                dh_own[here, :] = djn[:, :width]
                yield

            interleave([node_block(here) for here in node_rows], 1)
            if phase == 3:
                node_copy(2).start()
                low_start(2, 1)
            for job in before:
                job()
            dtotal, d4, d3, dn = (jnp.concatenate(x, axis=0) for x in (djs, d4s, d3s, dns))
            put_w(r, 6 * width, dot_tn(act_n[r], d4))
            put_w(r, 4 * width, dot_tn(jn[r], d3))
            put_v(r, 6, col_sum(dn * xh_n[r].astype(F32)))
            put_v(r, 7, col_sum(dn))
            put_v(r, 5, col_sum(d4.astype(F32)))
            put_v(r, 4, col_sum(d3.astype(F32)))
            gain = vec(r, 2)
            w2t = wc[r, 2 * width : 3 * width, :]
            wet = wc[r, 3 * width :, :]
            lo = lows[phase]
            sums = [jnp.zeros((8, width), F32)] * 3
            big_wait(phase - 1)

            def block(i):
                here = slice(i * n, (i + 1) * n)
                g = dot(es[here, col_r:col_1], dtotal)
                yield
                xh = xhs[r][here, :].astype(F32)
                inv = twice(invs[r][here, :].astype(F32))
                g = (de_ref[here, :].astype(F32) + g) * gain
                gx = g * xh
                d2 = inv * (g - row_mean(g) - xh * row_mean(gx))
                for k, value in enumerate((gx, g, d2)):
                    sums[k] = sums[k] + eight_rows(value)
                d2 = d2.astype(BF16)
                xhs[r][here, :] = d2
                yield
                d1 = dot(d2, w2t)
                yield
                d1 = (d1 * dds[r][here, :].astype(F32)).astype(BF16)
                dds[r][here, :] = d1
                yield
                back = dot(d1, wet)
                yield
                out = de_ref[here, :].astype(F32) + back
                big[here, :] = out
                lo[here, :] = out.astype(BF16)
                yield
                if (i + 1) * n % CHUNK == 0:
                    part = slice((i + 1) * n - CHUNK, (i + 1) * n)
                    big_copy(phase, i * n // CHUNK).start()
                    put_w(r, 3 * width, dot(acts[r][:, part], xhs[r][part, :]))
                    yield
                    for half in (slice(0, nodes), slice(nodes, 2 * nodes)):
                        add = dot(srt[half, part], dds[r][part, :])
                        acc[half, :] = add if part.start == 0 else acc[half, :] + add
                        yield
                    put_w(r, 0, dot_tn(es[part, own[r]], dds[r][part, :]))
                    yield

            interleave([block(i) for i in range(edges // n)], 1)
            low_start(phase, 0)
            both = jnp.concatenate([acc[:nodes, :], acc[nodes:, :]], axis=1).astype(BF16)
            node_copy(phase - 2).wait()

            def dn_out(here):
                out = dn_rows(here, True) + dh_own[here, :] + dot_nt(both[here, :], wsr)
                nodes_out(phase, here, out)
                return out

            def sums_out():
                put_v(r, 2, col_sum(sums[0]) / gain)
                put_v(r, 3, col_sum(sums[1]) / gain)
                put_v(r, 1, col_sum(sums[2]))
                put_v(r, 0, col_sum(both[:, width:].astype(F32)))

            def table_out():
                dws = dot_tn(jn[r, :, :width], both)
                put_w(r, width, dws[:, :width])
                put_w(r, 2 * width, dws[:, width:])

            return dn_out, (sums_out, table_out)

        forward(0, lambda here: h0_in[here, :].astype(F32))
        forward(1, lambda here: nf[0, here, :])
        load_cot.wait()
        low_copies(1)[0].wait()
        dn_out, jobs = backward(1, cot, lambda here, again=False: cotn[here, :].astype(F32), ())
        last = lambda here, again=False: nf[0, here, :] if again else dn_out(here)
        dn_out, jobs = backward(0, low, last, jobs)
        for here in node_rows:
            dn_out(here)
        node_copy(3).start()
        low_start(3, 1)
        for job in jobs:
            job()

        @pl.when(which == GRAPHS - 1)
        def _():
            drain()

        return carry

    lax.fori_loop(0, GRAPHS, graph, 0)
    wl = dd0.at[:GRAD_ROWS]

    for r in range(2):

        @pl.when(sec == r)
        def _(r=r):
            copy(wg.at[r], wg_keep, grad_sems.at[0]).start()

        @pl.when(sec != r)
        def _(r=r):
            wl[...] = wg[r].astype(BF16)
            copy(wl, wg_send, grad_sems.at[1]).start()

    copy(wg.at[0], wg_keep, grad_sems.at[0]).wait()
    copy(wl, wg_send, grad_sems.at[1]).wait()


def run_graphs(nodes, edges, sec, idx_s, idx_r, node, edge, ncot, ecot, w_mine, w_theirs, v_mine, v_theirs):
    width = node.shape[1]
    any_spec = pl.BlockSpec(memory_space=pl.ANY)
    vmem = pl.BlockSpec(memory_space=pltpu.VMEM)
    smem = pl.BlockSpec(memory_space=pltpu.SMEM)
    shape = jax.ShapeDtypeStruct
    whole = [shape((edge.shape[0], width), F32), shape((node.shape[0], width), F32)]
    outs = (
        *whole,
        *whole,
        shape((2, GRAPHS, edges, width), BF16),
        shape((2, GRAPHS, nodes, width), BF16),
        shape((GRAD_ROWS, width), F32),
        shape((GRAD_ROWS, width), BF16),
    )
    return pl.pallas_call(
        functools.partial(graphs_kernel, nodes, edges, width),
        out_shape=outs,
        in_specs=[smem, vmem, vmem] + [any_spec] * 6 + [vmem, vmem],
        out_specs=(any_spec,) * 8,
        scratch_shapes=[
            pltpu.VMEM((edges, 2 * width + 2 * nodes), BF16),
            pltpu.VMEM((2 * nodes, edges), BF16),
            *[pltpu.VMEM((edges, width), BF16)] * 2,
            *[pltpu.VMEM((width, edges), BF16)] * 2,
            *[pltpu.VMEM((edges, width), BF16)] * 4,
            *[pltpu.VMEM((edges, 128), BF16)] * 2,
            pltpu.VMEM((edges, width), F32),
            pltpu.VMEM((2, w_mine.shape[0], width), BF16),
            pltpu.VMEM((2, 4 * width, width), BF16),
            pltpu.VMEM((2, 8, width), F32),
            pltpu.VMEM((nodes, width), BF16),
            pltpu.VMEM((nodes, width), BF16),
            pltpu.VMEM((2, nodes, width), F32),
            pltpu.VMEM((2, nodes, width), BF16),
            pltpu.VMEM((2 * nodes, width), F32),
            pltpu.VMEM((nodes, width), F32),
            pltpu.VMEM((2 * nodes + width, width), BF16),
            pltpu.VMEM((2, nodes, 2 * width), BF16),
            *[pltpu.VMEM((2, nodes, width), BF16)] * 3,
            pltpu.VMEM((2, nodes, 128), F32),
            pltpu.VMEM((2, GRAD_ROWS, width), F32),
            pltpu.SemaphoreType.DMA((8,)),
            pltpu.SemaphoreType.DMA((edges // CHUNK,)),
            *[pltpu.SemaphoreType.DMA((4,))] * 3,
            pltpu.SemaphoreType.DMA((2,)),
        ],
        compiler_params=pltpu.CompilerParams(vmem_limit_bytes=60 * 2**20),
        cost_estimate=pl.CostEstimate(flops=80 * 2 * edges * width * width, transcendentals=0, bytes_accessed=2**25),
        name="graphs",
    )(sec, idx_s, idx_r, node, edge, ncot, ecot, w_mine, w_theirs, v_mine, v_theirs)


def spread_kernel(kind, nodes, edges, rows, sec_ref, recv_e, recv_n, *rest):
    out_e, out_n, e_in, n_in, e_out, n_out, in_sems, out_sems = rest[2:]
    start = GRAPHS * (1 - sec_ref[0])
    parts = []
    for g in range(GRAPHS):
        at = pl.multiple_of((start + g) * nodes, nodes)
        parts.append((recv_n.at[kind, g], n_in.at[g], n_out.at[g], out_n.at[pl.ds(at, nodes)]))
        for i in range(edges // rows):
            here = pl.ds(i * rows, rows)
            at = pl.multiple_of((start + g) * edges + i * rows, rows)
            parts.append((recv_e.at[kind, g, here], e_in.at[g, here], e_out.at[g, here], out_e.at[pl.ds(at, rows)]))
    reads = [pltpu.make_async_copy(p[0], p[1], in_sems.at[i]) for i, p in enumerate(parts)]
    writes = [pltpu.make_async_copy(p[2], p[3], out_sems.at[i]) for i, p in enumerate(parts)]
    for c in reads:
        c.start()
    for p, r, w in zip(parts, reads, writes):
        r.wait()
        p[2][...] = p[1][...].astype(F32)
        w.start()
    for w in writes:
        w.wait()


def spread(kind, nodes, edges, sec, recv_e, recv_n, full):
    width = recv_e.shape[-1]
    rows = 1024
    count = GRAPHS * (edges // rows + 1)
    any_spec = pl.BlockSpec(memory_space=pl.ANY)
    return pl.pallas_call(
        functools.partial(spread_kernel, kind, nodes, edges, rows),
        out_shape=tuple(jax.ShapeDtypeStruct(f.shape, f.dtype) for f in full),
        in_specs=[pl.BlockSpec(memory_space=pltpu.SMEM)] + [any_spec] * 4,
        out_specs=(any_spec,) * 2,
        input_output_aliases={3 + i: i for i in range(2)},
        scratch_shapes=[
            pltpu.VMEM((GRAPHS, edges, width), BF16),
            pltpu.VMEM((GRAPHS, nodes, width), BF16),
            pltpu.VMEM((GRAPHS, edges, width), F32),
            pltpu.VMEM((GRAPHS, nodes, width), F32),
            pltpu.SemaphoreType.DMA((count,)),
            pltpu.SemaphoreType.DMA((count,)),
        ],
        compiler_params=pltpu.CompilerParams(vmem_limit_bytes=24 * 2**20),
        cost_estimate=pl.CostEstimate(flops=0, transcendentals=0, bytes_accessed=12 * (edges + nodes) * width),
        name="spread",
    )(sec, recv_e, recv_n, *full)


def reduce_over_dp(pair, beside):
    devices = lax.axis_size("dp")
    sec = lax.axis_index("section")
    me = lax.axis_index("dp")
    bits = [1 << k for k in range(devices.bit_length() - 1)]
    orders = [bits, bits[:2][::-1] + bits[2:]]
    halved = min(2, len(bits))
    count = [0]

    def swap(part, step):
        pairs = [
            (s * devices + i, s * devices + (i ^ orders[s][step]))
            for s in range(2)
            for i in range(devices)
        ]
        part = part.astype(BF16)
        got = lax.ppermute(part, ("section", "dp"), pairs)
        if count[0] in beside:
            got = beside[count[0]](part, got)
        count[0] += 1
        return got.astype(F32)

    def high(step):
        return jnp.where(sec == 0, me // orders[0][step], me // orders[1][step]) % 2

    terms = pair
    for step in range(halved):
        half = terms[0].shape[0] // 2
        mine = high(step)
        keep = sum(lax.dynamic_slice_in_dim(t, mine * half, half, 0).astype(F32) for t in terms)
        send = sum(lax.dynamic_slice_in_dim(t, (1 - mine) * half, half, 0).astype(F32) for t in terms)
        part = keep + swap(send, step)
        terms = (part,)
    for step in range(halved, len(bits)):
        part = part + swap(part, step)
    for step in reversed(range(halved)):
        got = swap(part, step)
        if step == 0:
            return part, got, high(0)
        part = jnp.where(
            high(step) == 0, jnp.concatenate([part, got], 0), jnp.concatenate([got, part], 0)
        )
    rows = pair[0].shape[0] // 2
    return part[:rows], part[rows:], jnp.zeros((), jnp.int32)


def place_kernel(flag_ref, part_ref, got_ref, *outs):
    own = flag_ref[0] == 0
    rows = part_ref.shape[0]
    at = 0
    for out in outs:
        end = at + out.shape[0]
        if at < rows:
            stop = min(end, rows)
            out[: stop - at, :] = jnp.where(own, part_ref[at:stop, :], got_ref[at:stop, :])
        if end > rows:
            start = max(at, rows)
            here = slice(start - rows, end - rows)
            out[start - at :, :] = jnp.where(own, got_ref[here, :], part_ref[here, :])
        at = end


def place(part, got, flag, sizes):
    vmem = pl.BlockSpec(memory_space=pltpu.VMEM)
    return pl.pallas_call(
        place_kernel,
        out_shape=tuple(jax.ShapeDtypeStruct((rows, part.shape[1]), F32) for rows in sizes),
        in_specs=[pl.BlockSpec(memory_space=pltpu.SMEM), vmem, vmem],
        out_specs=(vmem,) * len(sizes),
        compiler_params=pltpu.CompilerParams(vmem_limit_bytes=16 * 2**20),
        name="place",
    )(flag.reshape(1).astype(jnp.int32), part, got)


def shards(
    node_input,
    edge_input,
    senders,
    receivers,
    node_cot,
    edge_cot,
    edge_w1,
    edge_b1,
    edge_w2,
    edge_b2,
    edge_gain,
    edge_shift,
    node_w1,
    node_b1,
    node_w2,
    node_b2,
    node_gain,
    node_shift,
):
    nodes = node_input.shape[0] // MICRO
    edges = edge_input.shape[0] // MICRO
    width = node_input.shape[1]
    sec = lax.axis_index("section").reshape(1).astype(jnp.int32)
    other = [(0, 1), (1, 0)]
    w_mine = jnp.concatenate([edge_w1[0], edge_w2[0], node_w1[0], node_w2[0]], axis=0)
    v_mine = jnp.concatenate(
        [edge_b1, edge_b2, edge_gain, edge_shift, node_b1, node_b2, node_gain, node_shift], axis=0
    )
    w_theirs = lax.ppermute(w_mine, "section", other)
    v_theirs = lax.ppermute(v_mine, "section", other)
    idx_s = senders.reshape(-1, 128)
    idx_r = receivers.reshape(-1, 128)
    out = run_graphs(
        nodes,
        edges,
        sec,
        idx_s,
        idx_r,
        node_input,
        edge_input,
        node_cot,
        edge_cot,
        w_mine,
        w_theirs,
        v_mine,
        v_theirs,
    )
    full = [out[:2], out[2:4]]
    came = lax.ppermute(out[7], "section", other)
    sent, came = lax.optimization_barrier((out[4:6], came))
    recv = tuple(lax.ppermute(x, "section", other) for x in sent)

    def fill(kind):
        def run(sent, came):
            sent, here, whole = lax.optimization_barrier((sent, recv, full[kind]))
            full[kind] = spread(kind, nodes, edges, sec, *here, whole)
            came, full[kind] = lax.optimization_barrier((came, full[kind]))
            return came

        return run

    total = reduce_over_dp((out[6], came), {3: fill(0), 5: fill(1)})
    (lat_e, lat_n), (gr_e, gr_n) = full
    out = place(*total, (3 * width, width, 2 * width, width) + (1,) * 8)
    w1, w2, n1, n2 = (w[None] for w in out[:4])
    return (
        lat_n[None],
        lat_e[None],
        gr_n[None],
        gr_e[None],
        w1,
        out[4],
        w2,
        out[5],
        out[6],
        out[7],
        n1,
        out[8],
        n2,
        out[9],
        out[10],
        out[11],
    )


def solution(mesh):
    rows = P("dp", None)
    mat = P("section", None, None)
    row = P("section", None)
    in_specs = (rows, rows, P("dp"), P("dp"), rows, rows) + (mat, row, mat, row, row, row) * 2
    whole = P("section", "dp", None)
    out_specs = (whole,) * 4 + (mat, row, mat, row, row, row) * 2
    return jax.shard_map(shards, mesh=mesh, in_specs=in_specs, out_specs=out_specs, check_vma=False)
```

profile of v0, /device:TPU:0, one launch (start us, length us, event | category | flops | bytes accessed | tf_op | source)
XLA Modules:
  0.0 135.8 jit_solution(10994440774077077959)
XLA Ops:
  0.6 1.3 pad_maximum_fusion.w_mine
  1.9 0.0 copy-start
  1.9 0.5 collective-permute-start
  2.5 0.8 concatenate.13.v_mine
  3.3 0.0 copy-start.1
  3.3 0.3 collective-permute-start.1
  3.6 1.0 collective-permute-done.1.v_theirs
  4.6 0.0 copy-start.4
  4.6 0.0 collective-permute-done.w_theirs
  4.6 0.0 copy-start.3
  4.6 0.0 copy-done
  4.6 0.0 copy-done.1
  4.6 0.6 copy-done.4
  5.2 0.3 copy-done.3
  5.5 73.5 %graphs.1 = (f32[16384,256]{1,0:T(8,128)}, f32[2048,256]{1,0:T(8,128)}, f32[16384,256]{1,0:T(8,128)}, f32[2048,256]{1,0:T(8,128)}, bf16[2,2,4096,256]{3,2,1,0:T(...) custom-call(s32[1]{0:T(128)} %bitcast.sec_ref, ...), custom_call_target="tpu_custom_call" | custom-call | flops 42949672960 | bytes 33554432 | tf_op jit(solution)/shard_map/graphs/pallas_call | solution.py:526
  79.0 0.8 collective-permute-start.2
  79.8 2.4 %collective-permute-done.2 = bf16[1856,256]{1,0:T(8,128)(2,1)S(1)} collective-permute-done((bf16[1856,256]{1,0:T(8,128)(2,1)}, bf16[1856,256]{1,0:T(8,128)(2,1)S(1)}, u32[]{:S(2)}, u32[]{:S(2)}) %collective-permute-start.2) | collective-permute-done | bytes 950304 | tf_op jit(solution)/shard_map/ppermute | solution.py:735
  82.2 0.4 collective-permute-start.7
  82.5 1.3 add_convert_fusion
  83.8 0.0 copy-start.2
  83.8 2.7 %collective-permute-start.3 = (bf16[928,256]{1,0:T(8,128)(2,1)S(1)}, bf16[928,256]{1,0:T(8,128)(2,1)S(1)}, u32[]{:S(2)}, u32[]{:S(2)}) collective-permute-start(bf16[928,256]{1,0:T(8,128)(2,1)S(1)} %add_convert_fusion), channel_id=1, source_target_pairs={{0,1},{1,0},{2,3},{3,2},{4,5},{5,4},{6,7},{7,6},{8,9},{9,8},{10,11... | collective-permute-start | bytes 1425416 | tf_op jit(solution)/shard_map/ppermute | solution.py:628
  86.5 6.6 %collective-permute-done.3 = bf16[928,256]{1,0:T(8,128)(2,1)S(1)} collective-permute-done((bf16[928,256]{1,0:T(8,128)(2,1)S(1)}, bf16[928,256]{1,0:T(8,128)(2,1)S(1)}, u32[]{:S(2)}, u32[]{:S(2)}) %collective-permute-start.3) | collective-permute-done | bytes 475168 | tf_op jit(solution)/shard_map/ppermute | solution.py:628
  93.1 1.3 convert_add_fusion
  94.5 2.1 %collective-permute-start.4 = (bf16[464,256]{1,0:T(8,128)(2,1)S(1)}, bf16[464,256]{1,0:T(8,128)(2,1)S(1)}, u32[]{:S(2)}, u32[]{:S(2)}) collective-permute-start(bf16[464,256]{1,0:T(8,128)(2,1)S(1)} %dynamic-slice_convert_fusion), channel_id=1, source_target_pairs={{0,2},{1,3},{2,0},{3,1},{4,6},{5,7},{6,4},{7,5},{8,10},{9,11},{10,... | collective-permute-start | bytes 712712 | tf_op jit(solution)/shard_map/ppermute | solution.py:628
  96.6 0.0 copy-done.2
  96.6 0.0 collective-permute-start.8
  96.6 4.1 %collective-permute-done.4 = bf16[464,256]{1,0:T(8,128)(2,1)S(1)} collective-permute-done((bf16[464,256]{1,0:T(8,128)(2,1)S(1)}, bf16[464,256]{1,0:T(8,128)(2,1)S(1)}, u32[]{:S(2)}, u32[]{:S(2)}) %collective-permute-start.4) | collective-permute-done | bytes 237600 | tf_op jit(solution)/shard_map/ppermute | solution.py:628
  100.7 0.1 fusion.1
  100.8 2.2 %collective-permute-start.5 = (bf16[464,256]{1,0:T(8,128)(2,1)S(1)}, bf16[464,256]{1,0:T(8,128)(2,1)S(1)}, u32[]{:S(2)}, u32[]{:S(2)}) collective-permute-start(bf16[464,256]{1,0:T(8,128)(2,1)S(1)} %fusion.1), channel_id=1, source_target_pairs={{0,4},{1,5},{2,6},{3,7},{4,0},{5,1},{6,2},{7,3},{8,12},{9,13},{10,... | collective-permute-start | bytes 712712 | tf_op jit(solution)/shard_map/ppermute | solution.py:628
  102.9 4.4 %collective-permute-done.5 = bf16[464,256]{1,0:T(8,128)(2,1)S(1)} collective-permute-done((bf16[464,256]{1,0:T(8,128)(2,1)S(1)}, bf16[464,256]{1,0:T(8,128)(2,1)S(1)}, u32[]{:S(2)}, u32[]{:S(2)}) %collective-permute-start.5) | collective-permute-done | bytes 237600 | tf_op jit(solution)/shard_map/ppermute | solution.py:628
  107.3 0.1 fusion
  107.4 2.8 %collective-permute-start.6 = (bf16[464,256]{1,0:T(8,128)(2,1)S(1)}, bf16[464,256]{1,0:T(8,128)(2,1)S(1)}, u32[]{:S(2)}, u32[]{:S(2)}) collective-permute-start(bf16[464,256]{1,0:T(8,128)(2,1)S(1)} %fusion), channel_id=1, source_target_pairs={{0,8},{1,9},{2,10},{3,11},{4,12},{5,13},{6,14},{7,15},{8,0},{9,1},... | collective-permute-start | bytes 712712 | tf_op jit(solution)/shard_map/ppermute | solution.py:628
  110.2 0.0 collective-permute-done.8.recv_n
  110.2 0.0 collective-permute-done.7.recv_e
  110.2 4.9 %spread.2 = (f32[16384,256]{1,0:T(8,128)}, f32[2048,256]{1,0:T(8,128)}) custom-call(s32[1]{0:T(128)} %bitcast.sec_ref, bf16[2,2,4096,256]{3,2,1,0:T(8,128)(2,1)} %collective-permute-done.7.recv_e, bf16[2,2,512,256]{3,2,1,0:T(8,128)(2,1)S(1)} %collective-permute-done.8.recv_n, ...), custom_call_target="tpu_custom_call", output_to_operand_aliasing={{0}: (3, {}), {1}: (4, {})} | custom-call | bytes 14155776 | tf_op jit(solution)/shard_map/spread/pallas_call | solution.py:592
  115.2 3.7 %collective-permute-done.6 = bf16[464,256]{1,0:T(8,128)(2,1)S(1)} collective-permute-done((bf16[464,256]{1,0:T(8,128)(2,1)S(1)}, bf16[464,256]{1,0:T(8,128)(2,1)S(1)}, u32[]{:S(2)}, u32[]{:S(2)}) %collective-permute-start.6) | collective-permute-done | bytes 237600 | tf_op jit(solution)/shard_map/ppermute | solution.py:628
  118.9 0.1 fusion.3
  119.1 1.2 collective-permute-start.9
  120.3 4.9 %collective-permute-done.9 = bf16[464,256]{1,0:T(8,128)(2,1)S(1)} collective-permute-done((bf16[464,256]{1,0:T(8,128)(2,1)S(1)}, bf16[464,256]{1,0:T(8,128)(2,1)S(1)}, u32[]{:S(2)}, u32[]{:S(2)}) %collective-permute-start.9) | collective-permute-done | bytes 237600 | tf_op jit(solution)/shard_map/ppermute | solution.py:628
  125.3 0.1 fusion.2
  125.4 1.2 collective-permute-start.10
  126.6 4.9 %spread.3 = (f32[16384,256]{1,0:T(8,128)}, f32[2048,256]{1,0:T(8,128)}) custom-call(s32[1]{0:T(128)} %bitcast.sec_ref, bf16[2,2,4096,256]{3,2,1,0:T(8,128)(2,1)} %collective-permute-done.7.recv_e, bf16[2,2,512,256]{3,2,1,0:T(8,128)(2,1)S(1)} %collective-permute-done.8.recv_n, ...), custom_call_target="tpu_custom_call", output_to_operand_aliasing={{0}: (3, {}), {1}: (4, {})} | custom-call | bytes 14155776 | tf_op jit(solution)/shard_map/spread/pallas_call | solution.py:592
  131.5 2.6 %collective-permute-done.10 = bf16[928,256]{1,0:T(8,128)(2,1)S(1)} collective-permute-done((bf16[928,256]{1,0:T(8,128)(2,1)S(1)}, bf16[928,256]{1,0:T(8,128)(2,1)S(1)}, u32[]{:S(2)}, u32[]{:S(2)}) %collective-permute-start.10) | collective-permute-done | bytes 475168 | tf_op jit(solution)/shard_map/ppermute | solution.py:628
  134.1 0.1 convert_element_type.55.got_ref
  134.2 1.4 %place.1 = (f32[768,256]{1,0:T(8,128)}, f32[256,256]{1,0:T(8,128)}, f32[512,256]{1,0:T(8,128)}, f32[256,256]{1,0:T(8,128)}, f32[1,256]{1,0:T(1,128)}, /*index=5*...) custom-call(s32[1]{0:T(128)} %bitcast.11.flag_ref, ...), custom_call_target="tpu_custom_call" | custom-call | tf_op jit(solution)/shard_map/place/pallas_call | solution.py:676
  (2 shorter events, 0.1 us)
Async XLA Ops:
  1.9 2.6 %copy-start = (bf16[1792,256]{1,0:T(8,128)(2,1)}, bf16[1792,256]{1,0:T(8,128)(2,1)S(1)}, u32[]{:S(2)}) copy-start(bf16[1792,256]{1,0:T(8,128)(2,1)S(1)} %pad_maximum_fusion.w_mine) | copy-start | bytes 2752516
  1.9 2.6 %collective-permute-start = (bf16[1792,256]{1,0:T(8,128)(2,1)S(1)}, bf16[1792,256]{1,0:T(8,128)(2,1)S(1)}, u32[]{:S(2)}, u32[]{:S(2)}) collective-permute-start(bf16[1792,256]{1,0:T(8,128)(2,1)S(1)} %pad_maximum_fusion.w_mine), channel_id=1, source_target_pairs={{0,16},{16,0},{1,17},{17,1},{2,18},{18,2},{3,19},{19,3},{4,20},{20... | collective-permute-start | bytes 2752520 | tf_op jit(solution)/shard_map/ppermute | solution.py:715
  3.3 1.3 copy-start.1
  3.3 1.3 collective-permute-start.1
  4.6 0.6 copy-start.4
  4.6 0.9 copy-start.3
  79.0 3.1 %collective-permute-start.2 = (bf16[1856,256]{1,0:T(8,128)(2,1)}, bf16[1856,256]{1,0:T(8,128)(2,1)S(1)}, u32[]{:S(2)}, u32[]{:S(2)}) collective-permute-start(bf16[1856,256]{1,0:T(8,128)(2,1)} %get-tuple-element.60), channel_id=1, source_target_pairs={{0,16},{16,0},{1,17},{17,1},{2,18},{18,2},{3,19},{19,3},{4,20},{20... | collective-permute-start | bytes 2850824 | tf_op jit(solution)/shard_map/ppermute | solution.py:735
  82.2 28.1 %collective-permute-start.7 = (bf16[2,2,4096,256]{3,2,1,0:T(8,128)(2,1)}, bf16[2,2,4096,256]{3,2,1,0:T(8,128)(2,1)}, u32[]{:S(2)}, u32[]{:S(2)}) collective-permute-start(bf16[2,2,4096,256]{3,2,1,0:T(8,128)(2,1)} %get-tuple-element.62), channel_id=1, source_target_pairs={{0,16},{16,0},{1,17},{17,1},{2,18},{18,2},{3,19},{19,3},{4,20},{20... | collective-permute-start | bytes 25165832 | tf_op jit(solution)/shard_map/ppermute | solution.py:737
  83.8 12.8 %copy-start.2 = (bf16[2,2,512,256]{3,2,1,0:T(8,128)(2,1)S(1)}, bf16[2,2,512,256]{3,2,1,0:T(8,128)(2,1)}, u32[]{:S(2)}) copy-start(bf16[2,2,512,256]{3,2,1,0:T(8,128)(2,1)} %get-tuple-element.63) | copy-start | bytes 3145732
  83.8 9.3 %collective-permute-start.3 = (bf16[928,256]{1,0:T(8,128)(2,1)S(1)}, bf16[928,256]{1,0:T(8,128)(2,1)S(1)}, u32[]{:S(2)}, u32[]{:S(2)}) collective-permute-start(bf16[928,256]{1,0:T(8,128)(2,1)S(1)} %add_convert_fusion), channel_id=1, source_target_pairs={{0,1},{1,0},{2,3},{3,2},{4,5},{5,4},{6,7},{7,6},{8,9},{9,8},{10,11... | collective-permute-start | bytes 1425416 | tf_op jit(solution)/shard_map/ppermute | solution.py:628
  94.5 6.2 %collective-permute-start.4 = (bf16[464,256]{1,0:T(8,128)(2,1)S(1)}, bf16[464,256]{1,0:T(8,128)(2,1)S(1)}, u32[]{:S(2)}, u32[]{:S(2)}) collective-permute-start(bf16[464,256]{1,0:T(8,128)(2,1)S(1)} %dynamic-slice_convert_fusion), channel_id=1, source_target_pairs={{0,2},{1,3},{2,0},{3,1},{4,6},{5,7},{6,4},{7,5},{8,10},{9,11},{10,... | collective-permute-start | bytes 712712 | tf_op jit(solution)/shard_map/ppermute | solution.py:628
  96.6 13.6 %collective-permute-start.8 = (bf16[2,2,512,256]{3,2,1,0:T(8,128)(2,1)S(1)}, bf16[2,2,512,256]{3,2,1,0:T(8,128)(2,1)S(1)}, u32[]{:S(2)}, u32[]{:S(2)}) collective-permute-start(bf16[2,2,512,256]{3,2,1,0:T(8,128)(2,1)S(1)} %copy-done.2), channel_id=1, source_target_pairs={{0,16},{16,0},{1,17},{17,1},{2,18},{18,2},{3,19},{19,3},{4,20},{20... | collective-permute-start | bytes 3145736 | tf_op jit(solution)/shard_map/ppermute | solution.py:737
  100.8 6.5 %collective-permute-start.5 = (bf16[464,256]{1,0:T(8,128)(2,1)S(1)}, bf16[464,256]{1,0:T(8,128)(2,1)S(1)}, u32[]{:S(2)}, u32[]{:S(2)}) collective-permute-start(bf16[464,256]{1,0:T(8,128)(2,1)S(1)} %fusion.1), channel_id=1, source_target_pairs={{0,4},{1,5},{2,6},{3,7},{4,0},{5,1},{6,2},{7,3},{8,12},{9,13},{10,... | collective-permute-start | bytes 712712 | tf_op jit(solution)/shard_map/ppermute | solution.py:628
  107.4 11.5 %collective-permute-start.6 = (bf16[464,256]{1,0:T(8,128)(2,1)S(1)}, bf16[464,256]{1,0:T(8,128)(2,1)S(1)}, u32[]{:S(2)}, u32[]{:S(2)}) collective-permute-start(bf16[464,256]{1,0:T(8,128)(2,1)S(1)} %fusion), channel_id=1, source_target_pairs={{0,8},{1,9},{2,10},{3,11},{4,12},{5,13},{6,14},{7,15},{8,0},{9,1},... | collective-permute-start | bytes 712712 | tf_op jit(solution)/shard_map/ppermute | solution.py:628
  119.1 6.2 %collective-permute-start.9 = (bf16[464,256]{1,0:T(8,128)(2,1)S(1)}, bf16[464,256]{1,0:T(8,128)(2,1)S(1)}, u32[]{:S(2)}, u32[]{:S(2)}) collective-permute-start(bf16[464,256]{1,0:T(8,128)(2,1)S(1)} %get-tuple-element.100), channel_id=1, source_target_pairs={{0,2},{1,3},{2,0},{3,1},{4,6},{5,7},{6,4},{7,5},{8,10},{9,11},{10,... | collective-permute-start | bytes 712712 | tf_op jit(solution)/shard_map/ppermute | solution.py:628
  125.4 8.7 %collective-permute-start.10 = (bf16[928,256]{1,0:T(8,128)(2,1)S(1)}, bf16[928,256]{1,0:T(8,128)(2,1)S(1)}, u32[]{:S(2)}, u32[]{:S(2)}) collective-permute-start(bf16[928,256]{1,0:T(8,128)(2,1)S(1)} %get-tuple-element.98), channel_id=1, source_target_pairs={{0,1},{1,0},{2,3},{3,2},{4,5},{5,4},{6,7},{7,6},{8,9},{9,8},{10,11... | collective-permute-start | bytes 1425416 | tf_op jit(solution)/shard_map/ppermute | solution.py:628
where the time goes:
time: 136 us
  Pallas kernels  84.8 us (62%)
  waiting for transfers between devices  29.6 us (22%)
  starting transfers between devices  14.2 us (10%)
  other arithmetic  4.38 us (3%)
  local copies, waits for them, and re-layouts  1.78 us (1%)
    pallas_call x1, Pallas kernels, run_graphs(): pl.pallas_call(functools.partial(graphs_kernel, nodes, edges, width), out...  73.5 us
    ppermute x6, waiting for transfers between devices, swap(): got = lax.ppermute(part, ('section', 'dp'), pairs)  26.3 us
    ppermute x6, starting transfers between devices, swap(): got = lax.ppermute(part, ('section', 'dp'), pairs)  12.2 us
    pallas_call x2, Pallas kernels, spread(): pl.pallas_call(functools.partial(spread_kernel, kind, nodes, edges, rows)...  9.89 us
  transfers between devices with their start and end apart: 11, of which 8 were waited for; matrix products, arithmetic and copies ran while one was open for 3% of the time, Pallas kernels for 7%

commit v1 on v0

--- a/solution.py
+++ b/solution.py
@@ -13,7 +13,7 @@
 BLOCK = 256
 NODE_BLOCKS = 1
 CHUNK = 1024
-GRAD_ROWS = 1856
+GRAD_ROWS = 1920
 F32 = jnp.float32
 BF16 = jnp.bfloat16
 
@@ -611,76 +611,77 @@
 
 def reduce_over_dp(pair, beside):
     devices = lax.axis_size("dp")
-    sec = lax.axis_index("section")
     me = lax.axis_index("dp")
-    bits = [1 << k for k in range(devices.bit_length() - 1)]
-    orders = [bits, bits[:2][::-1] + bits[2:]]
-    halved = min(2, len(bits))
     count = [0]
 
-    def swap(part, step):
-        pairs = [
-            (s * devices + i, s * devices + (i ^ orders[s][step]))
-            for s in range(2)
-            for i in range(devices)
+    def swap(parts, hops):
+        got = [
+            lax.ppermute(p.astype(BF16), "dp", [(i, i ^ hop) for i in range(devices)])
+            for p, hop in zip(parts, hops)
         ]
-        part = part.astype(BF16)
-        got = lax.ppermute(part, ("section", "dp"), pairs)
         if count[0] in beside:
-            got = beside[count[0]](part, got)
+            got[-1] = beside[count[0]](parts[-1], got[-1])
         count[0] += 1
-        return got.astype(F32)
-
-    def high(step):
-        return jnp.where(sec == 0, me // orders[0][step], me // orders[1][step]) % 2
-
-    terms = pair
-    for step in range(halved):
-        half = terms[0].shape[0] // 2
-        mine = high(step)
-        keep = sum(lax.dynamic_slice_in_dim(t, mine * half, half, 0).astype(F32) for t in terms)
-        send = sum(lax.dynamic_slice_in_dim(t, (1 - mine) * half, half, 0).astype(F32) for t in terms)
-        part = keep + swap(send, step)
-        terms = (part,)
-    for step in range(halved, len(bits)):
-        part = part + swap(part, step)
-    for step in reversed(range(halved)):
-        got = swap(part, step)
-        if step == 0:
-            return part, got, high(0)
-        part = jnp.where(
-            high(step) == 0, jnp.concatenate([part, got], 0), jnp.concatenate([got, part], 0)
+        return got
+
+    def scatter(terms, step):
+        place_of = (me // step) % 4
+        rows = terms[0].shape[0] // 4
+
+        def quarter(k):
+            at = (place_of ^ k) * rows
+            return sum(lax.dynamic_slice_in_dim(t, at, rows, 0).astype(F32) for t in terms)
+
+        got = swap([quarter(k) for k in (3, 1, 2)], (3 * step, step, 2 * step))
+        return quarter(0) + sum(g.astype(F32) for g in got)
+
+    part = scatter(pair, 1)
+    if devices >= 16:
+        part = scatter((part,), 4)
+    hop = 16 if devices >= 16 else 4
+    while hop < devices:
+        part = part + swap([part], (hop,))[0].astype(F32)
+        hop *= 2
+    part = part.astype(BF16)
+    if devices >= 16:
+        place_of = (me // 4) % 4
+        diagonal, one, two = swap([part] * 3, (12, 4, 8))
+        stack = jnp.stack([part, one, two, diagonal])
+        part = jnp.concatenate(
+            [lax.dynamic_index_in_dim(stack, place_of ^ q, 0, keepdims=False) for q in range(4)], axis=0
         )
-    rows = pair[0].shape[0] // 2
-    return part[:rows], part[rows:], jnp.zeros((), jnp.int32)
-
-
-def place_kernel(flag_ref, part_ref, got_ref, *outs):
-    own = flag_ref[0] == 0
-    rows = part_ref.shape[0]
-    at = 0
+    diagonal, one, two = swap([part] * 3, (3, 1, 2))
+    return (part, one, two, diagonal), me % 4
+
+
+def place_kernel(place_ref, *refs):
+    quarters, outs = refs[:4], refs[4:]
+    mine = place_ref[0]
+    rows = quarters[0].shape[0]
+    start = 0
     for out in outs:
-        end = at + out.shape[0]
-        if at < rows:
-            stop = min(end, rows)
-            out[: stop - at, :] = jnp.where(own, part_ref[at:stop, :], got_ref[at:stop, :])
-        if end > rows:
-            start = max(at, rows)
-            here = slice(start - rows, end - rows)
-            out[start - at :, :] = jnp.where(own, got_ref[here, :], part_ref[here, :])
-        at = end
-
-
-def place(part, got, flag, sizes):
+        end = start + out.shape[0]
+        for q in range(4):
+            at, stop = max(start, q * rows), min(end, (q + 1) * rows)
+            if at < stop:
+                here = slice(at - q * rows, stop - q * rows)
+                value = quarters[q][here, :]
+                for p in range(1, 4):
+                    value = jnp.where(mine == p, quarters[q ^ p][here, :], value)
+                out[at - start : stop - start, :] = value
+        start = end
+
+
+def place(quarters, place_of, sizes):
     vmem = pl.BlockSpec(memory_space=pltpu.VMEM)
     return pl.pallas_call(
         place_kernel,
-        out_shape=tuple(jax.ShapeDtypeStruct((rows, part.shape[1]), F32) for rows in sizes),
-        in_specs=[pl.BlockSpec(memory_space=pltpu.SMEM), vmem, vmem],
+        out_shape=tuple(jax.ShapeDtypeStruct((rows, quarters[0].shape[1]), F32) for rows in sizes),
+        in_specs=[pl.BlockSpec(memory_space=pltpu.SMEM)] + [vmem] * 4,
         out_specs=(vmem,) * len(sizes),
         compiler_params=pltpu.CompilerParams(vmem_limit_bytes=16 * 2**20),
         name="place",
-    )(flag.reshape(1).astype(jnp.int32), part, got)
+    )(place_of.reshape(1).astype(jnp.int32), *(q.astype(F32) for q in quarters))
 
 
 def shards(
@@ -745,9 +746,9 @@
 
         return run
 
-    total = reduce_over_dp((out[6], came), {3: fill(0), 5: fill(1)})
+    quarters, place_of = reduce_over_dp((out[6], came), {2: fill(0), 3: fill(1)})
     (lat_e, lat_n), (gr_e, gr_n) = full
-    out = place(*total, (3 * width, width, 2 * width, width) + (1,) * 8)
+    out = place(quarters, place_of, (3 * width, width, 2 * width, width) + (1,) * 8)
     w1, w2, n1, n2 = (w[None] for w in out[:4])
     return (
         lat_n[None],

time: 136 us -> 134 us (0.985)
  waiting for transfers between devices: 29.6 us -> 24 us
  starting transfers between devices: 14.2 us -> 17.9 us
    ppermute x6 -> x12, waiting for transfers between devices: 26.3 us -> 20.6 us  [swap(): lax.ppermute(p.astype(BF16), 'dp', [(i, i ^ hop) for i in range(devices)])]
    ppermute x6 -> x12, starting transfers between devices: 12.2 us -> 15.8 us  [swap(): lax.ppermute(p.astype(BF16), 'dp', [(i, i ^ hop) for i in range(devices)])]
  transfers between devices with their start and end apart: 11 -> 17, of which waited for: 8 -> 9; matrix products, arithmetic and copies ran while one was open for 3% -> 3% of each run, Pallas kernels for 7% -> 7%
where the time goes in v1:
time: 134 us
  Pallas kernels  85 us (63%)
  waiting for transfers between devices  24 us (18%)
  starting transfers between devices  17.9 us (13%)
  other arithmetic  4.14 us (3%)
  local copies, waits for them, and re-layouts  1.81 us (1%)
    pallas_call x1, Pallas kernels, run_graphs(): pl.pallas_call(functools.partial(graphs_kernel, nodes, edges, width), out...  73.6 us
    ppermute x12, waiting for transfers between devices, swap(): lax.ppermute(p.astype(BF16), 'dp', [(i, i ^ hop) for i in range(devices)])  20.6 us
    ppermute x12, starting transfers between devices, swap(): lax.ppermute(p.astype(BF16), 'dp', [(i, i ^ hop) for i in range(devices)])  15.8 us
    pallas_call x2, Pallas kernels, spread(): pl.pallas_call(functools.partial(spread_kernel, kind, nodes, edges, rows)...  9.89 us
  transfers between devices with their start and end apart: 17, of which 9 were waited for; matrix products, arithmetic and copies ran while one was open for 3% of the time, Pallas kernels for 7%

profile of v1, /device:TPU:0, one launch (start us, length us, event | category | flops | bytes accessed | tf_op | source)
XLA Modules:
  0.0 133.9 jit_solution(16962070120568447005)
XLA Ops:
  0.6 1.3 pad_maximum_fusion.w_mine
  1.9 0.0 copy-start
  1.9 0.5 collective-permute-start
  2.5 0.8 concatenate.10.v_mine
  3.3 0.3 collective-permute-start.1
  3.6 1.0 collective-permute-done.1.v_theirs
  4.6 0.0 collective-permute-done.w_theirs
  4.6 0.0 copy-done
  4.6 0.0 copy-done.1
  4.6 0.6 copy-done.3
  5.2 0.3 copy-done.2
  5.5 73.6 %graphs.1 = (f32[16384,256]{1,0:T(8,128)}, f32[2048,256]{1,0:T(8,128)}, f32[16384,256]{1,0:T(8,128)}, f32[2048,256]{1,0:T(8,128)}, bf16[2,2,4096,256]{3,2,1,0:T(...) custom-call(s32[1]{0:T(128)} %bitcast.sec_ref, ...), custom_call_target="tpu_custom_call" | custom-call | flops 42949672960 | bytes 33554432 | tf_op jit(solution)/shard_map/graphs/pallas_call | solution.py:526
  79.1 0.7 collective-permute-start.2
  79.8 2.4 %collective-permute-done.2 = bf16[1920,256]{1,0:T(8,128)(2,1)S(1)} collective-permute-done((bf16[1920,256]{1,0:T(8,128)(2,1)}, bf16[1920,256]{1,0:T(8,128)(2,1)S(1)}, u32[]{:S(2)}, u32[]{:S(2)}) %collective-permute-start.2) | collective-permute-done | bytes 983072 | tf_op jit(solution)/shard_map/ppermute | solution.py:736
  82.2 0.4 collective-permute-start.10
  82.6 0.1 collective-permute-start.11
  82.7 1.5 %add_convert_fusion.2 = (bf16[480,256]{1,0:T(8,128)(2,1)S(1)}, bf16[480,256]{1,0:T(8,128)(2,1)S(1)}, bf16[480,256]{1,0:T(8,128)(2,1)S(1)}) fusion(f32[1920,256]{1,0:T(8,128)} %get-tuple-element.57, s32[]{:T(128)S(6)} %select_n.64, bf16[1920,256]{1,0:T(8,128)(2,1)S(1)} %collective-permute-done.2, s32[]{:T(128)S(6)} %select_n.66, s32[]{:T(128)S(6)} %select_n.65), kind=kLoop, calls=%fused_computation.4 | loop fusion | flops 1105920 | bytes 2949132 | tf_op jit(solution)/shard_map/convert_element_type | solution.py:619
  84.2 3.6 %collective-permute-start.3 = (bf16[480,256]{1,0:T(8,128)(2,1)S(1)}, bf16[480,256]{1,0:T(8,128)(2,1)S(1)}, u32[]{:S(2)}, u32[]{:S(2)}) collective-permute-start(bf16[480,256]{1,0:T(8,128)(2,1)S(1)} %get-tuple-element.98), channel_id=1, source_target_pairs={{0,3},{1,2},{2,1},{3,0},{4,7},{5,6},{6,5},{7,4},{8,11},{9,10},{10,... | collective-permute-start | bytes 737288 | tf_op jit(solution)/shard_map/ppermute | solution.py:619
  87.9 0.5 collective-permute-start.5
  88.4 0.1 collective-permute-start.4
  88.5 6.2 %collective-permute-done.3 = bf16[480,256]{1,0:T(8,128)(2,1)S(1)} collective-permute-done((bf16[480,256]{1,0:T(8,128)(2,1)S(1)}, bf16[480,256]{1,0:T(8,128)(2,1)S(1)}, u32[]{:S(2)}, u32[]{:S(2)}) %collective-permute-start.3) | collective-permute-done | bytes 245792 | tf_op jit(solution)/shard_map/ppermute | solution.py:619
  94.7 4.9 %collective-permute-done.5 = bf16[480,256]{1,0:T(8,128)(2,1)S(1)} collective-permute-done((bf16[480,256]{1,0:T(8,128)(2,1)S(1)}, bf16[480,256]{1,0:T(8,128)(2,1)S(1)}, u32[]{:S(2)}, u32[]{:S(2)}) %collective-permute-start.5) | collective-permute-done | bytes 245792 | tf_op jit(solution)/shard_map/ppermute | solution.py:619
  99.6 0.3 collective-permute-done.4
  99.9 1.2 add_add_fusion
  101.1 3.7 %collective-permute-start.6 = (bf16[120,256]{1,0:T(8,128)(2,1)S(1)}, bf16[120,256]{1,0:T(8,128)(2,1)S(1)}, u32[]{:S(2)}, u32[]{:S(2)}) collective-permute-start(bf16[120,256]{1,0:T(8,128)(2,1)S(1)} %get-tuple-element.101), channel_id=1, source_target_pairs={{0,12},{1,13},{2,14},{3,15},{4,8},{5,9},{6,10},{7,11},{8,4},{9,5},... | collective-permute-start | bytes 184328 | tf_op jit(solution)/shard_map/ppermute | solution.py:619
  104.8 0.0 collective-permute-start.8
  104.8 0.8 collective-permute-start.7
  105.6 2.1 %collective-permute-done.6 = bf16[120,256]{1,0:T(8,128)(2,1)S(1)} collective-permute-done((bf16[120,256]{1,0:T(8,128)(2,1)S(1)}, bf16[120,256]{1,0:T(8,128)(2,1)S(1)}, u32[]{:S(2)}, u32[]{:S(2)}) %collective-permute-start.6) | collective-permute-done | bytes 61472 | tf_op jit(solution)/shard_map/ppermute | solution.py:619
  107.6 2.6 %collective-permute-done.8 = bf16[120,256]{1,0:T(8,128)(2,1)S(1)} collective-permute-done((bf16[120,256]{1,0:T(8,128)(2,1)S(1)}, bf16[120,256]{1,0:T(8,128)(2,1)S(1)}, u32[]{:S(2)}, u32[]{:S(2)}) %collective-permute-start.8) | collective-permute-done | bytes 61472 | tf_op jit(solution)/shard_map/ppermute | solution.py:619
  110.2 0.0 collective-permute-done.7
  110.3 1.8 %collective-permute-start.9 = (bf16[120,256]{1,0:T(8,128)(2,1)S(1)}, bf16[120,256]{1,0:T(8,128)(2,1)S(1)}, u32[]{:S(2)}, u32[]{:S(2)}) collective-permute-start(bf16[120,256]{1,0:T(8,128)(2,1)S(1)} %add_convert_fusion.3), channel_id=1, source_target_pairs={{0,8},{1,9},{2,10},{3,11},{4,12},{5,13},{6,14},{7,15},{8,0},{9,1},... | collective-permute-start | bytes 184328 | tf_op jit(solution)/shard_map/ppermute | solution.py:619
  112.0 1.7 %collective-permute-start.13 = (bf16[120,256]{1,0:T(8,128)(2,1)S(1)}, bf16[120,256]{1,0:T(8,128)(2,1)S(1)}, u32[]{:S(2)}, u32[]{:S(2)}) collective-permute-start(bf16[120,256]{1,0:T(8,128)(2,1)S(1)} %add_convert_fusion.3), channel_id=1, source_target_pairs={{0,12},{1,13},{2,14},{3,15},{4,8},{5,9},{6,10},{7,11},{8,4},{9,5},... | collective-permute-start | bytes 184328 | tf_op jit(solution)/shard_map/ppermute | solution.py:619
  113.8 0.0 collective-permute-start.12
  113.8 0.0 collective-permute-done.11.recv_n
  113.8 0.0 collective-permute-done.10.recv_e
  113.8 4.9 %spread.2 = (f32[16384,256]{1,0:T(8,128)}, f32[2048,256]{1,0:T(8,128)}) custom-call(s32[1]{0:T(128)} %bitcast.sec_ref, bf16[2,2,4096,256]{3,2,1,0:T(8,128)(2,1)} %collective-permute-done.10.recv_e, bf16[2,2,512,256]{3,2,1,0:T(8,128)(2,1)S(1)} %collective-permute-done.11.recv_n, ...), custom_call_target="tpu_custom_call", output_to_operand_aliasing={{0}: (3, {}), {1}: (4, {})} | custom-call | bytes 14155776 | tf_op jit(solution)/shard_map/spread/pallas_call | solution.py:592
  118.8 0.0 collective-permute-done.9
  118.8 0.0 collective-permute-done.13
  118.8 0.0 collective-permute-done.12
  118.9 0.1 fusion
  118.9 1.6 %collective-permute-start.14 = (bf16[480,256]{1,0:T(8,128)(2,1)S(1)}, bf16[480,256]{1,0:T(8,128)(2,1)S(1)}, u32[]{:S(2)}, u32[]{:S(2)}) collective-permute-start(bf16[480,256]{1,0:T(8,128)(2,1)S(1)} %get-tuple-element.105), channel_id=1, source_target_pairs={{0,2},{1,3},{2,0},{3,1},{4,6},{5,7},{6,4},{7,5},{8,10},{9,11},{10,... | collective-permute-start | bytes 737288 | tf_op jit(solution)/shard_map/ppermute | solution.py:619
  120.5 0.4 collective-permute-start.15
  120.9 1.6 %collective-permute-start.16 = (bf16[480,256]{1,0:T(8,128)(2,1)S(1)}, bf16[480,256]{1,0:T(8,128)(2,1)S(1)}, u32[]{:S(2)}, u32[]{:S(2)}) collective-permute-start(bf16[480,256]{1,0:T(8,128)(2,1)S(1)} %get-tuple-element.105), channel_id=1, source_target_pairs={{0,3},{1,2},{2,1},{3,0},{4,7},{5,6},{6,5},{7,4},{8,11},{9,10},{10,... | collective-permute-start | bytes 737288 | tf_op jit(solution)/shard_map/ppermute | solution.py:619
  122.5 4.9 %spread.3 = (f32[16384,256]{1,0:T(8,128)}, f32[2048,256]{1,0:T(8,128)}) custom-call(s32[1]{0:T(128)} %bitcast.sec_ref, bf16[2,2,4096,256]{3,2,1,0:T(8,128)(2,1)} %collective-permute-done.10.recv_e, bf16[2,2,512,256]{3,2,1,0:T(8,128)(2,1)S(1)} %collective-permute-done.11.recv_n, ...), custom_call_target="tpu_custom_call", output_to_operand_aliasing={{0}: (3, {}), {1}: (4, {})} | custom-call | bytes 14155776 | tf_op jit(solution)/shard_map/spread/pallas_call | solution.py:592
  127.5 0.0 collective-permute-done.14
  127.5 1.9 %collective-permute-done.15 = bf16[480,256]{1,0:T(8,128)(2,1)S(1)} collective-permute-done((bf16[480,256]{1,0:T(8,128)(2,1)S(1)}, bf16[480,256]{1,0:T(8,128)(2,1)S(1)}, u32[]{:S(2)}, u32[]{:S(2)}) %collective-permute-start.15) | collective-permute-done | bytes 245792 | tf_op jit(solution)/shard_map/ppermute | solution.py:619
  129.4 2.7 %collective-permute-done.16 = bf16[480,256]{1,0:T(8,128)(2,1)S(1)} collective-permute-done((bf16[480,256]{1,0:T(8,128)(2,1)S(1)}, bf16[480,256]{1,0:T(8,128)(2,1)S(1)}, u32[]{:S(2)}, u32[]{:S(2)}) %collective-permute-start.16) | collective-permute-done | bytes 245792 | tf_op jit(solution)/shard_map/ppermute | solution.py:619
  132.2 1.5 %place.1 = (f32[768,256]{1,0:T(8,128)}, f32[256,256]{1,0:T(8,128)}, f32[512,256]{1,0:T(8,128)}, f32[256,256]{1,0:T(8,128)}, f32[1,256]{1,0:T(1,128)}, /*index=5*...) custom-call(s32[1]{0:T(128)} %bitcast.19.place_ref, ...), custom_call_target="tpu_custom_call" | custom-call | tf_op jit(solution)/shard_map/place/pallas_call | solution.py:677
  (10 shorter events, 0.2 us)
Async XLA Ops:
  1.9 2.6 %copy-start = (bf16[1792,256]{1,0:T(8,128)(2,1)}, bf16[1792,256]{1,0:T(8,128)(2,1)S(1)}, u32[]{:S(2)}) copy-start(bf16[1792,256]{1,0:T(8,128)(2,1)S(1)} %pad_maximum_fusion.w_mine) | copy-start | bytes 2752516
  1.9 2.6 %collective-permute-start = (bf16[1792,256]{1,0:T(8,128)(2,1)S(1)}, bf16[1792,256]{1,0:T(8,128)(2,1)S(1)}, u32[]{:S(2)}, u32[]{:S(2)}) collective-permute-start(bf16[1792,256]{1,0:T(8,128)(2,1)S(1)} %pad_maximum_fusion.w_mine), channel_id=1, source_target_pairs={{0,16},{16,0},{1,17},{17,1},{2,18},{18,2},{3,19},{19,3},{4,20},{20... | collective-permute-start | bytes 2752520 | tf_op jit(solution)/shard_map/ppermute | solution.py:716
  3.3 1.3 copy-start.1
  3.3 1.3 collective-permute-start.1
  4.6 0.6 copy-start.3
  4.6 0.9 copy-start.2
  79.1 3.1 %collective-permute-start.2 = (bf16[1920,256]{1,0:T(8,128)(2,1)}, bf16[1920,256]{1,0:T(8,128)(2,1)S(1)}, u32[]{:S(2)}, u32[]{:S(2)}) collective-permute-start(bf16[1920,256]{1,0:T(8,128)(2,1)} %get-tuple-element.60), channel_id=1, source_target_pairs={{0,16},{16,0},{1,17},{17,1},{2,18},{18,2},{3,19},{19,3},{4,20},{20... | collective-permute-start | bytes 2949128 | tf_op jit(solution)/shard_map/ppermute | solution.py:736
  82.2 31.6 %collective-permute-start.10 = (bf16[2,2,4096,256]{3,2,1,0:T(8,128)(2,1)}, bf16[2,2,4096,256]{3,2,1,0:T(8,128)(2,1)}, u32[]{:S(2)}, u32[]{:S(2)}) collective-permute-start(bf16[2,2,4096,256]{3,2,1,0:T(8,128)(2,1)} %get-tuple-element.62), channel_id=1, source_target_pairs={{0,16},{16,0},{1,17},{17,1},{2,18},{18,2},{3,19},{19,3},{4,20},{20... | collective-permute-start | bytes 25165832 | tf_op jit(solution)/shard_map/ppermute | solution.py:738
  82.6 31.2 %collective-permute-start.11 = (bf16[2,2,512,256]{3,2,1,0:T(8,128)(2,1)}, bf16[2,2,512,256]{3,2,1,0:T(8,128)(2,1)S(1)}, u32[]{:S(2)}, u32[]{:S(2)}) collective-permute-start(bf16[2,2,512,256]{3,2,1,0:T(8,128)(2,1)} %get-tuple-element.63), channel_id=1, source_target_pairs={{0,16},{16,0},{1,17},{17,1},{2,18},{18,2},{3,19},{19,3},{4,20},{20... | collective-permute-start | bytes 3145736 | tf_op jit(solution)/shard_map/ppermute | solution.py:738
  84.2 10.5 %collective-permute-start.3 = (bf16[480,256]{1,0:T(8,128)(2,1)S(1)}, bf16[480,256]{1,0:T(8,128)(2,1)S(1)}, u32[]{:S(2)}, u32[]{:S(2)}) collective-permute-start(bf16[480,256]{1,0:T(8,128)(2,1)S(1)} %get-tuple-element.98), channel_id=1, source_target_pairs={{0,3},{1,2},{2,1},{3,0},{4,7},{5,6},{6,5},{7,4},{8,11},{9,10},{10,... | collective-permute-start | bytes 737288 | tf_op jit(solution)/shard_map/ppermute | solution.py:619
  87.9 11.7 %collective-permute-start.5 = (bf16[480,256]{1,0:T(8,128)(2,1)S(1)}, bf16[480,256]{1,0:T(8,128)(2,1)S(1)}, u32[]{:S(2)}, u32[]{:S(2)}) collective-permute-start(bf16[480,256]{1,0:T(8,128)(2,1)S(1)} %get-tuple-element.99), channel_id=1, source_target_pairs={{0,2},{1,3},{2,0},{3,1},{4,6},{5,7},{6,4},{7,5},{8,10},{9,11},{10,... | collective-permute-start | bytes 737288 | tf_op jit(solution)/shard_map/ppermute | solution.py:619
  88.4 11.5 %collective-permute-start.4 = (bf16[480,256]{1,0:T(8,128)(2,1)S(1)}, bf16[480,256]{1,0:T(8,128)(2,1)S(1)}, u32[]{:S(2)}, u32[]{:S(2)}) collective-permute-start(bf16[480,256]{1,0:T(8,128)(2,1)S(1)} %get-tuple-element.100), channel_id=1, source_target_pairs={{0,1},{1,0},{2,3},{3,2},{4,5},{5,4},{6,7},{7,6},{8,9},{9,8},{10,11... | collective-permute-start | bytes 737288 | tf_op jit(solution)/shard_map/ppermute | solution.py:619
  101.1 6.5 %collective-permute-start.6 = (bf16[120,256]{1,0:T(8,128)(2,1)S(1)}, bf16[120,256]{1,0:T(8,128)(2,1)S(1)}, u32[]{:S(2)}, u32[]{:S(2)}) collective-permute-start(bf16[120,256]{1,0:T(8,128)(2,1)S(1)} %get-tuple-element.101), channel_id=1, source_target_pairs={{0,12},{1,13},{2,14},{3,15},{4,8},{5,9},{6,10},{7,11},{8,4},{9,5},... | collective-permute-start | bytes 184328 | tf_op jit(solution)/shard_map/ppermute | solution.py:619
  104.8 5.4 %collective-permute-start.8 = (bf16[120,256]{1,0:T(8,128)(2,1)S(1)}, bf16[120,256]{1,0:T(8,128)(2,1)S(1)}, u32[]{:S(2)}, u32[]{:S(2)}) collective-permute-start(bf16[120,256]{1,0:T(8,128)(2,1)S(1)} %get-tuple-element.102), channel_id=1, source_target_pairs={{0,8},{1,9},{2,10},{3,11},{4,12},{5,13},{6,14},{7,15},{8,0},{9,1},... | collective-permute-start | bytes 184328 | tf_op jit(solution)/shard_map/ppermute | solution.py:619
  104.8 5.4 %collective-permute-start.7 = (bf16[120,256]{1,0:T(8,128)(2,1)S(1)}, bf16[120,256]{1,0:T(8,128)(2,1)S(1)}, u32[]{:S(2)}, u32[]{:S(2)}) collective-permute-start(bf16[120,256]{1,0:T(8,128)(2,1)S(1)} %get-tuple-element.103), channel_id=1, source_target_pairs={{0,4},{1,5},{2,6},{3,7},{4,0},{5,1},{6,2},{7,3},{8,12},{9,13},{10,... | collective-permute-start | bytes 184328 | tf_op jit(solution)/shard_map/ppermute | solution.py:619
  110.3 8.5 %collective-permute-start.9 = (bf16[120,256]{1,0:T(8,128)(2,1)S(1)}, bf16[120,256]{1,0:T(8,128)(2,1)S(1)}, u32[]{:S(2)}, u32[]{:S(2)}) collective-permute-start(bf16[120,256]{1,0:T(8,128)(2,1)S(1)} %add_convert_fusion.3), channel_id=1, source_target_pairs={{0,8},{1,9},{2,10},{3,11},{4,12},{5,13},{6,14},{7,15},{8,0},{9,1},... | collective-permute-start | bytes 184328 | tf_op jit(solution)/shard_map/ppermute | solution.py:619
  112.0 6.7 %collective-permute-start.13 = (bf16[120,256]{1,0:T(8,128)(2,1)S(1)}, bf16[120,256]{1,0:T(8,128)(2,1)S(1)}, u32[]{:S(2)}, u32[]{:S(2)}) collective-permute-start(bf16[120,256]{1,0:T(8,128)(2,1)S(1)} %add_convert_fusion.3), channel_id=1, source_target_pairs={{0,12},{1,13},{2,14},{3,15},{4,8},{5,9},{6,10},{7,11},{8,4},{9,5},... | collective-permute-start | bytes 184328 | tf_op jit(solution)/shard_map/ppermute | solution.py:619
  113.8 5.0 %collective-permute-start.12 = (bf16[120,256]{1,0:T(8,128)(2,1)S(1)}, bf16[120,256]{1,0:T(8,128)(2,1)S(1)}, u32[]{:S(2)}, u32[]{:S(2)}) collective-permute-start(bf16[120,256]{1,0:T(8,128)(2,1)S(1)} %add_convert_fusion.3), channel_id=1, source_target_pairs={{0,4},{1,5},{2,6},{3,7},{4,0},{5,1},{6,2},{7,3},{8,12},{9,13},{10,... | collective-permute-start | bytes 184328 | tf_op jit(solution)/shard_map/ppermute | solution.py:619
  118.9 8.5 %collective-permute-start.14 = (bf16[480,256]{1,0:T(8,128)(2,1)S(1)}, bf16[480,256]{1,0:T(8,128)(2,1)S(1)}, u32[]{:S(2)}, u32[]{:S(2)}) collective-permute-start(bf16[480,256]{1,0:T(8,128)(2,1)S(1)} %get-tuple-element.105), channel_id=1, source_target_pairs={{0,2},{1,3},{2,0},{3,1},{4,6},{5,7},{6,4},{7,5},{8,10},{9,11},{10,... | collective-permute-start | bytes 737288 | tf_op jit(solution)/shard_map/ppermute | solution.py:619
  120.5 8.9 %collective-permute-start.15 = (bf16[480,256]{1,0:T(8,128)(2,1)S(1)}, bf16[480,256]{1,0:T(8,128)(2,1)S(1)}, u32[]{:S(2)}, u32[]{:S(2)}) collective-permute-start(bf16[480,256]{1,0:T(8,128)(2,1)S(1)} %get-tuple-element.105), channel_id=1, source_target_pairs={{0,1},{1,0},{2,3},{3,2},{4,5},{5,4},{6,7},{7,6},{8,9},{9,8},{10,11... | collective-permute-start | bytes 737288 | tf_op jit(solution)/shard_map/ppermute | solution.py:619
  120.9 11.2 %collective-permute-start.16 = (bf16[480,256]{1,0:T(8,128)(2,1)S(1)}, bf16[480,256]{1,0:T(8,128)(2,1)S(1)}, u32[]{:S(2)}, u32[]{:S(2)}) collective-permute-start(bf16[480,256]{1,0:T(8,128)(2,1)S(1)} %get-tuple-element.105), channel_id=1, source_target_pairs={{0,3},{1,2},{2,1},{3,0},{4,7},{5,6},{6,5},{7,4},{8,11},{9,10},{10,... | collective-permute-start | bytes 737288 | tf_op jit(solution)/shard_map/ppermute | solution.py:619
